TPU v7x, 32 devices: a whole 2x2x4 slice. The times are simulated.
32 devices in a mesh: lat: 4 (over y, core), lon: 8 (over z, x).
Axes of the slice: x: 2, y: 2, z: 4, core: 2. Of those that a mesh axis runs over, the one named last changes fastest.
Arguments:
- observation_residual: bfloat16 [128, 16384], P(None, ('lat', 'lon')), may hold values from -6 to 6
- obs_index: int32 [2, 16384], P(None, ('lat', 'lon')), may hold values from 0 to 8191, as said below
- obs_count: int32 [1, 1024], P(None, ('lat', 'lon')), may hold values from 12 to 16, as said below
- obs_weight: float32 [128], replicated, may hold values from 0.3 to 3
- jacobian: bfloat16 [128, 8, 137], replicated, may hold values from -0.5 to 0.5
- decoder: bfloat16 [137, 128], replicated, may hold values from -0.5 to 0.5
- conv_weight: bfloat16 [4, 3, 128, 128], replicated, may hold values from -0.3125 to 0.3125
- gates: bfloat16 [4, 128, 512, 512], P(None, None, 'lon', 'lat'), may hold values from 0.049804688 to 1.09375
- encoder: bfloat16 [128, 137], replicated, may hold values from -0.5 to 0.5
Outputs:
- state_grad: float32 [137, 512, 512], P(None, 'lon', 'lat')
Inputs may be any that keep to these rules, and one draw needn't show every extreme that they name: `obs_index`: row 0 is a column within the destination tile, longitude offset * 128 + latitude offset, up to 8191; row 1 is a Jacobian block below 8. `obs_count`: slots of a pair at or after its count are unused. In every draw some tiles receive 16 from every sender.
All inputs are finite; a program needn't handle non-finite values.
Results may differ from a plain program's by a relative error of at most 0.0056.
Values may be sent and summed in bfloat16 or wider, within the bound.
A program may use at most 128 MiB of HBM per device.

v0:
```python
import jax
import jax.numpy as jnp
from jax import lax
from jax.sharding import PartitionSpec as P


def with_halo(block, sides, width):
    for axis, dim in sides:
        count = lax.axis_size(axis)
        forward = [(i, i + 1) for i in range(count - 1)]
        forward.append((count - 1, 0))
        backward = [(target, source) for source, target in forward]
        low = lax.ppermute(
            lax.slice_in_dim(block, block.shape[dim] - width, None, axis=dim), axis, forward
        )
        high = lax.ppermute(lax.slice_in_dim(block, 0, width, axis=dim), axis, backward)
        block = jnp.concatenate([low, block, high], axis=dim)
    return block


def project(resid, kinds, counts, obs_weight, jacobian, slot_index):
    channels, kind_count, vertical_levels = jacobian.shape
    senders = counts.shape[0]
    slot_grid = (
        jnp.arange(senders * slot_index, dtype=jnp.int32).reshape(senders, slot_index) % slot_index
    )
    valid = (slot_grid < counts[:, None]).reshape(-1)
    weighted = jnp.where(
        valid[None, :], obs_weight[:, None] * resid.astype(jnp.float32), 0.0
    ).astype(jnp.bfloat16)
    jac_flat = jacobian.reshape(channels, kind_count * vertical_levels)
    every_kind = lax.dot_general(
        jac_flat, weighted, (((0,), (0,)), ((), ())), preferred_element_type=jnp.float32
    )
    every_kind = every_kind.reshape(kind_count, vertical_levels, -1)
    picked = (kinds[None, :] == jnp.arange(kind_count, dtype=jnp.int32)[:, None]).astype(
        jnp.float32
    )
    return jnp.sum(every_kind * picked[:, None, :], axis=0).astype(jnp.bfloat16)


def per_device(
    observation_residual,
    obs_index,
    obs_count,
    obs_weight,
    jacobian,
    decoder,
    conv_weight,
    gates,
    encoder,
):
    lat_count = lax.axis_size("lat")
    lon_count = lax.axis_size("lon")
    device_count = lat_count * lon_count
    slot_count = observation_residual.shape[1]
    slot_index = slot_count // device_count
    vertical_levels = jacobian.shape[2]
    layers_n, width, tile_lon, tile_lat = gates.shape
    cell_total = tile_lon * tile_lat
    incr = project(
        observation_residual, obs_index[1], obs_count[0], obs_weight, jacobian, slot_index
    )
    incr_in, cells_in = (
        lax.all_to_all(
            lax.all_to_all(
                incr.reshape(vertical_levels, lat_count, lon_count, slot_index),
                "lat",
                split_axis=1,
                concat_axis=1,
                tiled=True,
            ),
            "lon",
            split_axis=2,
            concat_axis=2,
            tiled=True,
        ),
        lax.all_to_all(
            lax.all_to_all(
                obs_index[0:1].reshape(1, lat_count, lon_count, slot_index),
                "lat",
                split_axis=1,
                concat_axis=1,
                tiled=True,
            ),
            "lon",
            split_axis=2,
            concat_axis=2,
            tiled=True,
        ),
    )
    incr_in = incr_in.reshape(vertical_levels, slot_count)
    cells_in = cells_in.reshape(1, slot_count)
    block_tensor = 512
    cell_ids = jnp.arange(cell_total, dtype=jnp.int32)

    def accumulate_block(step, total):
        incr_part = lax.dynamic_slice_in_dim(incr_in, step * block_tensor, block_tensor, 1)
        cell_part = lax.dynamic_slice_in_dim(cells_in[0], step * block_tensor, block_tensor, 0)
        onehot = (cell_part[:, None] == cell_ids[None, :]).astype(jnp.bfloat16)
        return total + jnp.dot(incr_part, onehot, preferred_element_type=jnp.float32)

    column_grad = lax.fori_loop(
        0,
        slot_count // block_tensor,
        accumulate_block,
        jnp.zeros((vertical_levels, cell_total), jnp.float32),
    )
    hidden = lax.dot_general(
        decoder,
        column_grad.astype(jnp.bfloat16),
        (((0,), (0,)), ((), ())),
        preferred_element_type=jnp.float32,
    )
    for layer in reversed(range(layers_n)):
        field = hidden.astype(jnp.bfloat16).reshape(width, tile_lon, tile_lat)
        padded = with_halo(field, (("lon", 1),), 4)
        back = jnp.zeros((width, cell_total), jnp.float32)
        for tap in range(3):
            offset = 8 - 4 * tap
            window = padded[:, offset : offset + tile_lon, :].reshape(width, cell_total)
            back = back + lax.dot_general(
                conv_weight[layer, tap],
                window,
                (((0,), (0,)), ((), ())),
                preferred_element_type=jnp.float32,
            )
        hidden = hidden + gates[layer].reshape(width, cell_total) * back
    state_grad = column_grad + lax.dot_general(
        encoder,
        hidden.astype(jnp.bfloat16),
        (((0,), (0,)), ((), ())),
        preferred_element_type=jnp.float32,
    )
    return state_grad.reshape(vertical_levels, tile_lon, tile_lat)


def solution(mesh):
    return jax.shard_map(
        per_device,
        mesh=mesh,
        in_specs=(
            P(None, ("lat", "lon")),
            P(None, ("lat", "lon")),
            P(None, ("lat", "lon")),
            P(),
            P(),
            P(),
            P(),
            P(None, None, "lon", "lat"),
            P(),
        ),
        out_specs=P(None, "lon", "lat"),
        check_vma=False,
    )
```

profile of v0, /device:TPU:0, one launch (start us, length us, event | category | flops | bytes accessed | tf_op | source)
XLA Modules:
  0.0 146.9 jit_solution(12924634530774949210)
XLA Ops:
  0.0 0.8 slice_reduce_fusion
  1.5 4.2 %all-to-all-start.2 = ((s32[4,1,128]{2,1,0:T(1,128)}), s32[4,1,128]{2,1,0:T(1,128)S(1)}, u32[]{:S(2)}, u32[]{:S(2)}) async-start(s32[4,1,128]{2,1,0:T(1,128)} %reshape.168), calls=%async_computation.2 | async-start | bytes 4096 | tf_op jit(solution)/shard_map/all_to_all | solution.py:79
  5.8 1.0 copy.28
  6.9 0.7 lt.28
  7.8 2.8 %convolution_bitcast_fusion.2 = f32[1096,512]{1,0:T(8,128)} fusion(bf16[128,1096]{0,1:T(8,128)(2,1)S(1)} %reshape.136, bf16[128,512]{1,0:T(8,128)(2,1)} %param.9, f32[128]{0:T(128)} %param.12, pred[512]{0:T(512)(128)(4,1)S(1)} %fusion.60), kind=kOutput, calls=%fused_computation.27 | convolution fusion | flops 143917056 | bytes 2657280 | tf_op jit(solution)/shard_map/dot_general | solution.py:32
  10.6 1.9 %reshape.137 = f32[8,137,512]{2,1,0:T(8,128)S(1)} reshape(f32[1096,512]{1,0:T(8,128)} %convolution_bitcast_fusion.2) | data formatting | bytes 4489216 | tf_op jit(solution)/shard_map/reshape | solution.py:35
  12.8 0.8 copy.29
  13.7 3.4 %all-to-all-start = ((bf16[137,4,8,16]{0,3,2,1:T(8,128)(2,1)}), bf16[137,4,8,16]{0,3,2,1:T(8,128)(2,1)S(1)}, u32[]{:S(2)}, u32[]{:S(2)}) async-start(bf16[137,4,8,16]{0,3,2,1:T(8,128)(2,1)} %bitcast.3), calls=%async_computation | async-start | bytes 524288 | tf_op jit(solution)/shard_map/all_to_all | solution.py:66
  18.9 4.1 %all-to-all-done = bf16[137,4,8,16]{0,3,2,1:T(8,128)(2,1)S(1)} async-done(((bf16[137,4,8,16]{0,3,2,1:T(8,128)(2,1)}), bf16[137,4,8,16]{0,3,2,1:T(8,128)(2,1)S(1)}, u32[]{:S(2)}, u32[]{:S(2)}) %all-to-all-start) | async-done | bytes 140320 | tf_op jit(solution)/shard_map/all_to_all | solution.py:66
  23.1 6.2 %all-to-all-start.3 = ((s32[1,4,8,16]{3,1,0,2:T(4,128)}), s32[1,4,8,16]{3,1,0,2:T(4,128)S(1)}, u32[]{:S(2)}, u32[]{:S(2)}) async-start(s32[1,4,8,16]{3,1,0,2:T(4,128)} %copy.32), calls=%async_computation.3 | async-start | bytes 32768 | tf_op jit(solution)/shard_map/all_to_all | solution.py:78
  29.3 0.7 copy.30
  30.0 5.9 %all-to-all-done.3 = s32[1,4,8,16]{3,1,0,2:T(4,128)S(1)} async-done(((s32[1,4,8,16]{3,1,0,2:T(4,128)}), s32[1,4,8,16]{3,1,0,2:T(4,128)S(1)}, u32[]{:S(2)}, u32[]{:S(2)}) %all-to-all-start.3) | async-done | bytes 2080 | tf_op jit(solution)/shard_map/all_to_all | solution.py:78
  35.9 3.4 %all-to-all-start.1 = ((bf16[137,4,8,16]{0,3,1,2:T(8,128)(2,1)}), bf16[137,4,8,16]{0,3,1,2:T(8,128)(2,1)S(1)}, u32[]{:S(2)}, u32[]{:S(2)}) async-start(bf16[137,4,8,16]{0,3,1,2:T(8,128)(2,1)} %copy.30), calls=%async_computation.1 | async-start | bytes 524288 | tf_op jit(solution)/shard_map/all_to_all | solution.py:65
  39.3 10.1 %slice_convert_fusion = (f32[1,128,64,128]{3,2,1,0:T(8,128)}, f32[1,128,64,128]{3,2,1,0:T(8,128)}, f32[1,128,64,128]{3,2,1,0:T(8,128)}, f32[1,128,64,128]{3,2,1,0:T(8,128)}) fusion(bf16[4,128,64,128]{3,2,1,0:T(8,128)(2,1)} %param.16), kind=kLoop, calls=%fused_computation.38 | loop fusion | flops 4194304 | bytes 25165824 | tf_op jit(solution)/shard_map/convert_element_type | solution.py:128
  49.4 5.5 %copy.34 = f32[1,128,64,128]{1,3,2,0:T(8,128)} copy(f32[1,128,64,128]{3,2,1,0:T(8,128)} %get-tuple-element.17) | data formatting | bytes 8388608 | tf_op jit(solution)/shard_map/convert_element_type | solution.py:128
  54.9 5.4 %copy.35 = f32[1,128,64,128]{1,3,2,0:T(8,128)} copy(f32[1,128,64,128]{3,2,1,0:T(8,128)} %get-tuple-element.16) | data formatting | bytes 8388608 | tf_op jit(solution)/shard_map/convert_element_type | solution.py:128
  60.3 5.4 %copy.36 = f32[1,128,64,128]{1,3,2,0:T(8,128)} copy(f32[1,128,64,128]{3,2,1,0:T(8,128)} %get-tuple-element.24) | data formatting | bytes 8388608 | tf_op jit(solution)/shard_map/convert_element_type | solution.py:128
  65.8 5.4 %copy.37 = f32[1,128,64,128]{1,3,2,0:T(8,128)} copy(f32[1,128,64,128]{3,2,1,0:T(8,128)} %get-tuple-element.15) | data formatting | bytes 8388608 | tf_op jit(solution)/shard_map/convert_element_type | solution.py:128
  71.3 3.8 %fusion = f32[137,8192]{1,0:T(8,128)S(1)} fusion(bf16[137,512]{0,1:T(8,128)(2,1)S(1)} %bitcast.146, s32[512]{0:T(512)S(1)} %eq.47), kind=kOutput, calls=%fused_computation.1 | convolution fusion | flops 1153433600 | bytes 4631552 | tf_op jit(solution)/shard_map/while/body/eval_jaxpr/dot_general | solution.py:101
  75.2 1.4 fusion.66
  76.5 0.8 copy-done.2
  77.3 4.7 %collective-permute-start = (bf16[128,4,128]{0,2,1:T(8,128)(2,1)S(1)}, bf16[128,4,128]{0,2,1:T(8,128)(2,1)S(1)}, u32[]{:S(2)}, u32[]{:S(2)}) collective-permute-start(bf16[128,4,128]{0,2,1:T(8,128)(2,1)S(1)} %get-tuple-element.41), channel_id=1, source_target_pairs={{1,0},{2,1},{3,2},{4,3},{5,4},{6,5},{7,6},{0,7},{9,8},{10,9},{11,1... | collective-permute-start | bytes 393224 | tf_op jit(solution)/shard_map/ppermute | solution.py:16
  82.0 0.7 fusion.42
  82.7 1.8 %collective-permute-done = bf16[128,4,128]{0,2,1:T(8,128)(2,1)S(1)} collective-permute-done((bf16[128,4,128]{0,2,1:T(8,128)(2,1)S(1)}, bf16[128,4,128]{0,2,1:T(8,128)(2,1)S(1)}, u32[]{:S(2)}, u32[]{:S(2)}) %collective-permute-start) | collective-permute-done | bytes 131104 | tf_op jit(solution)/shard_map/ppermute | solution.py:16
  84.6 5.1 %collective-permute-done.1 = bf16[128,4,128]{0,2,1:T(8,128)(2,1)S(1)} collective-permute-done((bf16[128,4,128]{0,2,1:T(8,128)(2,1)S(1)}, bf16[128,4,128]{0,2,1:T(8,128)(2,1)S(1)}, u32[]{:S(2)}, u32[]{:S(2)}) %collective-permute-start.1) | collective-permute-done | bytes 131104 | tf_op jit(solution)/shard_map/ppermute | solution.py:13
  90.1 0.7 fusion.40
  90.8 1.5 %copy-done.5 = f32[1,128,64,128]{1,3,2,0:T(8,128)S(1)} copy-done((f32[1,128,64,128]{1,3,2,0:T(8,128)S(1)}, f32[1,128,64,128]{1,3,2,0:T(8,128)}, u32[]{:S(2)}) %copy-start.5) | copy-done | bytes 4194328
  92.3 1.3 fusion.67
  93.6 2.0 %collective-permute-start.3 = (bf16[128,4,128]{0,2,1:T(8,128)(2,1)S(1)}, bf16[128,4,128]{0,2,1:T(8,128)(2,1)S(1)}, u32[]{:S(2)}, u32[]{:S(2)}) collective-permute-start(bf16[128,4,128]{0,2,1:T(8,128)(2,1)S(1)} %get-tuple-element.38), channel_id=1, source_target_pairs={{0,1},{1,2},{2,3},{3,4},{4,5},{5,6},{6,7},{7,0},{8,9},{9,10},{10,1... | collective-permute-start | bytes 393224 | tf_op jit(solution)/shard_map/ppermute | solution.py:13
  96.3 2.3 %collective-permute-done.2 = bf16[128,4,128]{0,2,1:T(8,128)(2,1)S(1)} collective-permute-done((bf16[128,4,128]{0,2,1:T(8,128)(2,1)S(1)}, bf16[128,4,128]{0,2,1:T(8,128)(2,1)S(1)}, u32[]{:S(2)}, u32[]{:S(2)}) %collective-permute-start.2) | collective-permute-done | bytes 131104 | tf_op jit(solution)/shard_map/ppermute | solution.py:16
  98.6 2.8 %collective-permute-done.3 = bf16[128,4,128]{0,2,1:T(8,128)(2,1)S(1)} collective-permute-done((bf16[128,4,128]{0,2,1:T(8,128)(2,1)S(1)}, bf16[128,4,128]{0,2,1:T(8,128)(2,1)S(1)}, u32[]{:S(2)}, u32[]{:S(2)}) %collective-permute-start.3) | collective-permute-done | bytes 131104 | tf_op jit(solution)/shard_map/ppermute | solution.py:13
  101.7 0.7 fusion.35
  102.4 1.5 %copy-done.4 = f32[1,128,64,128]{1,3,2,0:T(8,128)S(1)} copy-done((f32[1,128,64,128]{1,3,2,0:T(8,128)S(1)}, f32[1,128,64,128]{1,3,2,0:T(8,128)}, u32[]{:S(2)}) %copy-start.4) | copy-done | bytes 4194328
  103.9 1.3 fusion.68
  105.3 2.0 %collective-permute-start.5 = (bf16[128,4,128]{0,2,1:T(8,128)(2,1)S(1)}, bf16[128,4,128]{0,2,1:T(8,128)(2,1)S(1)}, u32[]{:S(2)}, u32[]{:S(2)}) collective-permute-start(bf16[128,4,128]{0,2,1:T(8,128)(2,1)S(1)} %get-tuple-element.34), channel_id=1, source_target_pairs={{0,1},{1,2},{2,3},{3,4},{4,5},{5,6},{6,7},{7,0},{8,9},{9,10},{10,1... | collective-permute-start | bytes 393224 | tf_op jit(solution)/shard_map/ppermute | solution.py:13
  107.3 0.7 fusion.32
  108.0 2.3 %collective-permute-done.4 = bf16[128,4,128]{0,2,1:T(8,128)(2,1)S(1)} collective-permute-done((bf16[128,4,128]{0,2,1:T(8,128)(2,1)S(1)}, bf16[128,4,128]{0,2,1:T(8,128)(2,1)S(1)}, u32[]{:S(2)}, u32[]{:S(2)}) %collective-permute-start.4) | collective-permute-done | bytes 131104 | tf_op jit(solution)/shard_map/ppermute | solution.py:16
  110.2 2.8 %collective-permute-done.5 = bf16[128,4,128]{0,2,1:T(8,128)(2,1)S(1)} collective-permute-done((bf16[128,4,128]{0,2,1:T(8,128)(2,1)S(1)}, bf16[128,4,128]{0,2,1:T(8,128)(2,1)S(1)}, u32[]{:S(2)}, u32[]{:S(2)}) %collective-permute-start.5) | collective-permute-done | bytes 131104 | tf_op jit(solution)/shard_map/ppermute | solution.py:13
  113.4 0.7 fusion.30
  114.1 1.5 %copy-done.3 = f32[1,128,64,128]{1,3,2,0:T(8,128)S(1)} copy-done((f32[1,128,64,128]{1,3,2,0:T(8,128)S(1)}, f32[1,128,64,128]{1,3,2,0:T(8,128)}, u32[]{:S(2)}) %copy-start.3) | copy-done | bytes 4194328
  115.6 3.3 %fusion.69 = (bf16[128,8192]{0,1:T(8,128)(2,1)S(1)}, f32[128,8192]{0,1:T(8,128)}) fusion(f32[128,8192]{0,1:T(8,128)S(1)} %get-tuple-element.50, f32[128,8192]{0,1:T(8,128)S(1)} %bitcast.134, f32[8192,128]{1,0:T(8,128)S(1)} %fusion.30, f32[8192,128]{1,0:T(8,128)S(1)} %fusion.32, bf16[128,8192]{0,1:T(8,128)(2,1)S(1)} %bitcast.144, ...), kind=kOutput, calls=%fused_computation.95 | convolution fusion | flops 273678336 | bytes 25198592 | tf_op jit(solution)/shard_map/dot_general | solution.py:122
  119.0 2.0 %collective-permute-start.7 = (bf16[128,4,128]{0,2,1:T(8,128)(2,1)S(1)}, bf16[128,4,128]{0,2,1:T(8,128)(2,1)S(1)}, u32[]{:S(2)}, u32[]{:S(2)}) collective-permute-start(bf16[128,4,128]{0,2,1:T(8,128)(2,1)S(1)} %get-tuple-element.30), channel_id=1, source_target_pairs={{0,1},{1,2},{2,3},{3,4},{4,5},{5,6},{6,7},{7,0},{8,9},{9,10},{10,1... | collective-permute-start | bytes 393224 | tf_op jit(solution)/shard_map/ppermute | solution.py:13
  121.0 2.7 %fusion.26 = f32[8192,128]{1,0:T(8,128)} fusion(bf16[128,8192]{0,1:T(8,128)(2,1)S(1)} %get-tuple-element.51, bf16[4,3,128,128]{3,2,1,0:T(8,128)(2,1)S(1)} %copy-done.6), kind=kOutput, calls=%fused_computation.48 | convolution fusion | flops 268435456 | bytes 6324224 | tf_op jit(solution)/shard_map/dot_general | solution.py:122
  123.9 3.0 %collective-permute-done.7 = bf16[128,4,128]{0,2,1:T(8,128)(2,1)S(1)} collective-permute-done((bf16[128,4,128]{0,2,1:T(8,128)(2,1)S(1)}, bf16[128,4,128]{0,2,1:T(8,128)(2,1)S(1)}, u32[]{:S(2)}, u32[]{:S(2)}) %collective-permute-start.7) | collective-permute-done | bytes 131104 | tf_op jit(solution)/shard_map/ppermute | solution.py:13
  127.3 2.6 %fusion.24 = f32[8192,128]{1,0:T(8,128)} fusion(bf16[128,8192]{0,1:T(8,128)(2,1)S(1)} %bitcast.141, bf16[4,3,128,128]{3,2,1,0:T(8,128)(2,1)S(1)} %copy-done.6), kind=kOutput, calls=%fused_computation.46 | convolution fusion | flops 268435456 | bytes 6324224 | tf_op jit(solution)/shard_map/dot_general | solution.py:122
  129.9 11.0 %fusion.1 = f32[137,8192]{1,0:T(8,128)} fusion(f32[137,8192]{1,0:T(8,128)} %copy-done.2, bf16[128,137]{0,1:T(8,128)(2,1)S(1)} %copy-done.7, f32[128,8192]{0,1:T(8,128)} %get-tuple-element.52, f32[128,8192]{0,1:T(8,128)} %bitcast.137, f32[8192,128]{1,0:T(8,128)} %fusion.24, f32[8192,128]{1,0:T(8,128)} %fusion.26, bf16[128,8192]{0,1:T(8,128)(2,1)S(1)} %bitcast.145, ...), kind=kOutput, calls=%fused_computation.3 | convolution fusion | flops 562110464 | bytes 27922432 | tf_op jit(solution)/shard_map/dot_general | solution.py:129
  140.9 3.2 %copy.38 = f32[18,8,64,128]{3,2,1,0:T(8,128)S(1)} copy(f32[18,8,64,128]{3,1,2,0:T(8,128)} %bitcast.132) | data formatting | bytes 9437184
  144.1 2.8 %slice.152 = f32[137,64,128]{2,1,0:T(8,128)} slice(f32[144,64,128]{2,1,0:T(8,128)S(1)} %bitcast.133), slice={[0:137], [0:64], [0:128]} | slice | bytes 8978432 | tf_op jit(solution)/shard_map/reshape | solution.py:135
  (44 shorter events, 6.0 us)
Async XLA Ops:
  0.0 75.1 %copy-start = (bf16[137,128]{1,0:T(8,128)(2,1)S(1)}, bf16[137,128]{1,0:T(8,128)(2,1)}, u32[]{:S(2)}) copy-start(bf16[137,128]{1,0:T(8,128)(2,1)} %param.14) | copy-start | bytes 105220
  1.5 12.1 %all-to-all-start.2 = ((s32[4,1,128]{2,1,0:T(1,128)}), s32[4,1,128]{2,1,0:T(1,128)S(1)}, u32[]{:S(2)}, u32[]{:S(2)}) async-start(s32[4,1,128]{2,1,0:T(1,128)} %reshape.168), calls=%async_computation.2 | async-start | bytes 4096 | tf_op jit(solution)/shard_map/all_to_all | solution.py:79
  13.7 9.4 %all-to-all-start = ((bf16[137,4,8,16]{0,3,2,1:T(8,128)(2,1)}), bf16[137,4,8,16]{0,3,2,1:T(8,128)(2,1)S(1)}, u32[]{:S(2)}, u32[]{:S(2)}) async-start(bf16[137,4,8,16]{0,3,2,1:T(8,128)(2,1)} %bitcast.3), calls=%async_computation | async-start | bytes 524288 | tf_op jit(solution)/shard_map/all_to_all | solution.py:66
  23.1 12.8 %all-to-all-start.3 = ((s32[1,4,8,16]{3,1,0,2:T(4,128)}), s32[1,4,8,16]{3,1,0,2:T(4,128)S(1)}, u32[]{:S(2)}, u32[]{:S(2)}) async-start(s32[1,4,8,16]{3,1,0,2:T(4,128)} %copy.32), calls=%async_computation.3 | async-start | bytes 32768 | tf_op jit(solution)/shard_map/all_to_all | solution.py:78
  35.9 35.4 %all-to-all-start.1 = ((bf16[137,4,8,16]{0,3,1,2:T(8,128)(2,1)}), bf16[137,4,8,16]{0,3,1,2:T(8,128)(2,1)S(1)}, u32[]{:S(2)}, u32[]{:S(2)}) async-start(bf16[137,4,8,16]{0,3,1,2:T(8,128)(2,1)} %copy.30), calls=%async_computation.1 | async-start | bytes 524288 | tf_op jit(solution)/shard_map/all_to_all | solution.py:65
  75.2 2.1 %copy-start.2 = (f32[137,8192]{1,0:T(8,128)}, f32[137,8192]{1,0:T(8,128)S(1)}, u32[]{:S(2)}) copy-start(f32[137,8192]{1,0:T(8,128)S(1)} %fusion) | copy-start | bytes 13467652
  75.2 6.9 %copy-start.6 = (bf16[4,3,128,128]{3,2,1,0:T(8,128)(2,1)S(1)}, bf16[4,3,128,128]{3,2,1,0:T(8,128)(2,1)}, u32[]{:S(2)}) copy-start(bf16[4,3,128,128]{3,2,1,0:T(8,128)(2,1)} %param.15) | copy-start | bytes 1179652
  77.3 7.2 %collective-permute-start = (bf16[128,4,128]{0,2,1:T(8,128)(2,1)S(1)}, bf16[128,4,128]{0,2,1:T(8,128)(2,1)S(1)}, u32[]{:S(2)}, u32[]{:S(2)}) collective-permute-start(bf16[128,4,128]{0,2,1:T(8,128)(2,1)S(1)} %get-tuple-element.41), channel_id=1, source_target_pairs={{1,0},{2,1},{3,2},{4,3},{5,4},{6,5},{7,6},{0,7},{9,8},{10,9},{11,1... | collective-permute-start | bytes 393224 | tf_op jit(solution)/shard_map/ppermute | solution.py:16
  82.0 7.7 %collective-permute-start.1 = (bf16[128,4,128]{0,2,1:T(8,128)(2,1)S(1)}, bf16[128,4,128]{0,2,1:T(8,128)(2,1)S(1)}, u32[]{:S(2)}, u32[]{:S(2)}) collective-permute-start(bf16[128,4,128]{0,2,1:T(8,128)(2,1)S(1)} %get-tuple-element.42), channel_id=1, source_target_pairs={{0,1},{1,2},{2,3},{3,4},{4,5},{5,6},{6,7},{7,0},{8,9},{9,10},{10,1... | collective-permute-start | bytes 393224 | tf_op jit(solution)/shard_map/ppermute | solution.py:13
  90.1 2.2 %copy-start.5 = (f32[1,128,64,128]{1,3,2,0:T(8,128)S(1)}, f32[1,128,64,128]{1,3,2,0:T(8,128)}, u32[]{:S(2)}) copy-start(f32[1,128,64,128]{1,3,2,0:T(8,128)} %copy.34) | copy-start | bytes 12582916
  93.6 5.0 %collective-permute-start.2 = (bf16[128,4,128]{0,2,1:T(8,128)(2,1)S(1)}, bf16[128,4,128]{0,2,1:T(8,128)(2,1)S(1)}, u32[]{:S(2)}, u32[]{:S(2)}) collective-permute-start(bf16[128,4,128]{0,2,1:T(8,128)(2,1)S(1)} %get-tuple-element.37), channel_id=1, source_target_pairs={{1,0},{2,1},{3,2},{4,3},{5,4},{6,5},{7,6},{0,7},{9,8},{10,9},{11,1... | collective-permute-start | bytes 393224 | tf_op jit(solution)/shard_map/ppermute | solution.py:16
  93.6 7.7 %collective-permute-start.3 = (bf16[128,4,128]{0,2,1:T(8,128)(2,1)S(1)}, bf16[128,4,128]{0,2,1:T(8,128)(2,1)S(1)}, u32[]{:S(2)}, u32[]{:S(2)}) collective-permute-start(bf16[128,4,128]{0,2,1:T(8,128)(2,1)S(1)} %get-tuple-element.38), channel_id=1, source_target_pairs={{0,1},{1,2},{2,3},{3,4},{4,5},{5,6},{6,7},{7,0},{8,9},{9,10},{10,1... | collective-permute-start | bytes 393224 | tf_op jit(solution)/shard_map/ppermute | solution.py:13
  101.7 2.2 %copy-start.4 = (f32[1,128,64,128]{1,3,2,0:T(8,128)S(1)}, f32[1,128,64,128]{1,3,2,0:T(8,128)}, u32[]{:S(2)}) copy-start(f32[1,128,64,128]{1,3,2,0:T(8,128)} %copy.35) | copy-start | bytes 12582916
  105.2 5.0 %collective-permute-start.4 = (bf16[128,4,128]{0,2,1:T(8,128)(2,1)S(1)}, bf16[128,4,128]{0,2,1:T(8,128)(2,1)S(1)}, u32[]{:S(2)}, u32[]{:S(2)}) collective-permute-start(bf16[128,4,128]{0,2,1:T(8,128)(2,1)S(1)} %get-tuple-element.33), channel_id=1, source_target_pairs={{1,0},{2,1},{3,2},{4,3},{5,4},{6,5},{7,6},{0,7},{9,8},{10,9},{11,1... | collective-permute-start | bytes 393224 | tf_op jit(solution)/shard_map/ppermute | solution.py:16
  105.3 7.7 %collective-permute-start.5 = (bf16[128,4,128]{0,2,1:T(8,128)(2,1)S(1)}, bf16[128,4,128]{0,2,1:T(8,128)(2,1)S(1)}, u32[]{:S(2)}, u32[]{:S(2)}) collective-permute-start(bf16[128,4,128]{0,2,1:T(8,128)(2,1)S(1)} %get-tuple-element.34), channel_id=1, source_target_pairs={{0,1},{1,2},{2,3},{3,4},{4,5},{5,6},{6,7},{7,0},{8,9},{9,10},{10,1... | collective-permute-start | bytes 393224 | tf_op jit(solution)/shard_map/ppermute | solution.py:13
  113.4 2.2 %copy-start.3 = (f32[1,128,64,128]{1,3,2,0:T(8,128)S(1)}, f32[1,128,64,128]{1,3,2,0:T(8,128)}, u32[]{:S(2)}) copy-start(f32[1,128,64,128]{1,3,2,0:T(8,128)} %copy.36) | copy-start | bytes 12582916
  118.9 5.0 %collective-permute-start.6 = (bf16[128,4,128]{0,2,1:T(8,128)(2,1)S(1)}, bf16[128,4,128]{0,2,1:T(8,128)(2,1)S(1)}, u32[]{:S(2)}, u32[]{:S(2)}) collective-permute-start(bf16[128,4,128]{0,2,1:T(8,128)(2,1)S(1)} %get-tuple-element.29), channel_id=1, source_target_pairs={{1,0},{2,1},{3,2},{4,3},{5,4},{6,5},{7,6},{0,7},{9,8},{10,9},{11,1... | collective-permute-start | bytes 393224 | tf_op jit(solution)/shard_map/ppermute | solution.py:16
  119.0 7.9 %collective-permute-start.7 = (bf16[128,4,128]{0,2,1:T(8,128)(2,1)S(1)}, bf16[128,4,128]{0,2,1:T(8,128)(2,1)S(1)}, u32[]{:S(2)}, u32[]{:S(2)}) collective-permute-start(bf16[128,4,128]{0,2,1:T(8,128)(2,1)S(1)} %get-tuple-element.30), channel_id=1, source_target_pairs={{0,1},{1,2},{2,3},{3,4},{4,5},{5,6},{6,7},{7,0},{8,9},{9,10},{10,1... | collective-permute-start | bytes 393224 | tf_op jit(solution)/shard_map/ppermute | solution.py:13
  127.3 2.7 %copy-start.7 = (bf16[128,137]{0,1:T(8,128)(2,1)S(1)}, bf16[128,137]{0,1:T(8,128)(2,1)}, u32[]{:S(2)}) copy-start(bf16[128,137]{0,1:T(8,128)(2,1)} %param.17) | copy-start | bytes 105220
  144.1 2.8 %copy-start.1 = (bf16[137,128]{1,0:T(8,128)(2,1)S(1)}, bf16[137,128]{1,0:T(8,128)(2,1)}, u32[]{:S(2)}) copy-start(bf16[137,128]{1,0:T(8,128)(2,1)} %param.14) | copy-start | bytes 105220
where the time goes:
time: 148 us; the launch traced here: 147 us
  local copies, waits for them, and re-layouts  41.4 us (28%)
  matrix products  34.3 us (23%)
  waiting for transfers between devices  30.2 us (20%)
  starting transfers between devices  28.2 us (19%)
  other arithmetic  12.6 us (9%)
    convert_element_type x4, local copies, waits for them, and re-layouts, per_device(): hidden = hidden + gates[layer].reshape(width, cell_total) * back  21.8 us
    dot_general x11, matrix products, per_device(): lax.dot_general(conv_weight[layer, tap], window, (((0,), (0,)), ((), ()))...  15.3 us
    ppermute x4, waiting for transfers between devices, with_halo(): lax.ppermute(lax.slice_in_dim(block, block.shape[dim] - width, None, axis...  13.7 us
    dot_general x1, matrix products, per_device(): lax.dot_general(encoder, hidden.astype(jnp.bfloat16), (((0,), (0,)), ((),...  11 us
    unnamed x20, local copies, waits for them, and re-layouts  10.2 us
    convert_element_type x1, other arithmetic, per_device(): hidden = hidden + gates[layer].reshape(width, cell_total) * back  10.1 us
    ppermute x4, waiting for transfers between devices, with_halo(): lax.ppermute(lax.slice_in_dim(block, 0, width, axis=dim), axis, backward)  6.57 us
    all_to_all x1, starting transfers between devices, per_device(): lax.all_to_all(lax.all_to_all(obs_index[0:1].reshape(1, lat_count, lon_co...  6.21 us
  transfers between devices with their start and end apart: 12, of which 10 were waited for; matrix products, arithmetic and copies ran while one was open for 32% of the time, Pallas kernels for 0%

commit v1 on v0

v1 whole, which is shorter than its diff:
```python
import functools

import jax
import jax.numpy as jnp
from jax import lax
from jax.experimental import pallas as pl
from jax.experimental.pallas import tpu as pltpu
from jax.sharding import PartitionSpec as P

MESH = pl.DeviceIdType.MESH
F32 = jnp.float32
BF16 = jnp.bfloat16


def up(value, unit):
    return (value + unit - 1) // unit * unit


def kernel(
    dims,
    resid, index, counts, weight, jac, dec, conv, enc, gates, out,
    sent, got, incr, place, cg, hid, field, stage, gate, taps, dec_t, enc_t, tall, wide, done,
    a2a_send, a2a_recv, halo_send, halo_recv, gate_sem, out_sem,
):
    lat_n, lon_n, slot, kinds_n, levels, layers, width, tile_lon, tile_lat = dims
    devices = lat_n * lon_n
    lev = incr.shape[0]
    quads = tile_lon // 4
    my_lat, my_lon = lax.axis_index("lat"), lax.axis_index("lon")
    me = my_lat * lon_n + my_lon
    right, left = lax.rem(my_lon + 1, lon_n), lax.rem(my_lon + lon_n - 1, lon_n)

    def gate_copy(layer):
        return pltpu.make_async_copy(gates.at[layer], stage.at[layer % 2], gate_sem.at[layer % 2])

    order = list(reversed(range(layers)))
    for layer in order[:2]:
        gate_copy(layer).start()

    barrier = pltpu.get_barrier_semaphore()

    @pl.loop(1, devices)
    def _(off):
        d = lax.rem(me + off, devices)
        pl.semaphore_signal(
            barrier, inc=1, device_id=(d // lon_n, lax.rem(d, lon_n)), device_id_type=MESH
        )

    weight_lanes = jnp.transpose(jnp.broadcast_to(weight[...], (128, weight.shape[1])))
    counts8 = jnp.broadcast_to(counts[...].astype(F32), (8, devices)).astype(BF16)

    @pl.loop(0, devices * slot // 128)
    def _(chunk):
        lanes = pl.ds(pl.multiple_of(chunk * 128, 128), 128)
        pair = (lax.broadcasted_iota(jnp.int32, (devices, 128), 1) + chunk * 128) // slot
        owner = lax.broadcasted_iota(jnp.int32, (devices, 128), 0)
        spread = jnp.where(pair == owner, 1.0, 0.0).astype(BF16)
        limit = jnp.dot(counts8, spread, preferred_element_type=F32)[0:1]
        nth = lax.broadcasted_iota(jnp.int32, (1, 128), 1) % slot
        used = nth.astype(F32) < limit
        weighted = jnp.where(used, weight_lanes * resid[:, lanes].astype(F32), 0.0)
        kinds = index[1:2, lanes]
        cells = index[0:1, lanes]
        rows = [
            jnp.where(kinds == k, weighted, 0.0).astype(BF16) for k in range(kinds_n)
        ]
        row = lax.broadcasted_iota(jnp.int32, (16, 128), 0)
        lon = (cells // tile_lat).astype(F32)
        lat = (cells % tile_lat).astype(F32)
        rows.append(jnp.where(row == 0, lon, jnp.where(row == 1, lat, 0.0)).astype(BF16))
        stack = jnp.concatenate(rows, axis=0)
        sent[lanes, :] = lax.dot_general(
            stack, jac[...], (((0,), (0,)), ((), ())), preferred_element_type=F32
        ).astype(BF16)

    pl.semaphore_wait(barrier, devices - 1)

    mine = pl.ds(pl.multiple_of(me * slot, slot), slot)

    def slots_to(d):
        return pltpu.make_async_remote_copy(
            src_ref=sent.at[pl.ds(pl.multiple_of(d * slot, slot), slot)],
            dst_ref=got.at[mine],
            send_sem=a2a_send.at[d],
            recv_sem=a2a_recv.at[me],
            device_id=(d // lon_n, lax.rem(d, lon_n)),
            device_id_type=MESH,
        )

    def slots_from(s):
        return pltpu.make_async_remote_copy(
            src_ref=sent.at[mine],
            dst_ref=got.at[pl.ds(pl.multiple_of(s * slot, slot), slot)],
            send_sem=a2a_send.at[s],
            recv_sem=a2a_recv.at[s],
            device_id=(s // lon_n, lax.rem(s, lon_n)),
            device_id_type=MESH,
        )

    @pl.loop(1, devices)
    def _(off):
        slots_to(lax.rem(me + off, devices)).start()

    got[mine, :] = sent[mine, :]

    for layer in range(layers):
        for tap in range(3):
            taps[layer, :, (2 - tap) * width : (3 - tap) * width] = jnp.transpose(
                conv[layer, tap].astype(F32)
            ).astype(BF16)
    tall[...] = jnp.zeros_like(tall)
    tall[0:levels, :] = dec[...].astype(F32)
    dec_t[...] = jnp.transpose(tall[...])[:, 0:lev].astype(BF16)
    wide[...] = jnp.zeros_like(wide)
    wide[:, 0:levels] = enc[...].astype(F32)
    enc_t[...] = jnp.transpose(wide[...])[0:lev].astype(BF16)

    for at, layer in enumerate(order):
        gate_copy(layer).wait()

        @pl.loop(0, width // 4)
        def _(block):
            for part in range(4):
                c = block * 4 + part
                rows = pl.ds(pl.multiple_of(c * tile_lon, tile_lon), tile_lon)
                gate[layer, rows, :] = stage[layer % 2, c].astype(F32)

        if at + 2 < layers:
            gate_copy(order[at + 2]).start()

    @pl.loop(1, devices)
    def _(off):
        s = lax.rem(me + devices - off, devices)
        slots_from(s).wait_recv()

    @pl.loop(0, devices * slot // 128)
    def _(chunk):
        lanes = pl.ds(pl.multiple_of(chunk * 128, 128), 128)
        block = got[lanes, :].astype(F32)
        incr[:, lanes] = jnp.transpose(block)[0:lev].astype(BF16)
        lane = lax.broadcasted_iota(jnp.int32, (128, tile_lat), 1).astype(F32)
        at_lat = block[:, levels + 1 : levels + 2] == lane
        place[lanes, :] = jnp.where(at_lat, block[:, levels : levels + 1], -1.0).astype(BF16)

    def rows_of(q):
        return pl.ds(pl.multiple_of(q * width, width), width)

    def halos(layer, rp):
        to_right = pltpu.make_async_remote_copy(
            src_ref=field.at[layer, rp, rows_of(quads)],
            dst_ref=field.at[layer, rp, rows_of(0)],
            send_sem=halo_send.at[layer, rp, 0],
            recv_sem=halo_recv.at[layer, rp, 0],
            device_id=(my_lat, right),
            device_id_type=MESH,
        )
        to_left = pltpu.make_async_remote_copy(
            src_ref=field.at[layer, rp, rows_of(1)],
            dst_ref=field.at[layer, rp, rows_of(quads + 1)],
            send_sem=halo_send.at[layer, rp, 1],
            recv_sem=halo_recv.at[layer, rp, 1],
            device_id=(my_lat, left),
            device_id_type=MESH,
        )
        return to_right, to_left

    def scatter(rp, q):
        lon = 4 * (q - 1) + 2 * rp
        hot = []
        for r in range(2):
            value = jnp.full((1, tile_lat), lon + r, jnp.int32).astype(F32).astype(BF16)
            hot.append(jnp.where(place[...] == value, 1.0, 0.0).astype(BF16))
        total = jnp.dot(incr[...], jnp.concatenate(hot, axis=1), preferred_element_type=F32)
        cg[rp, q - 1] = total
        hidden = jnp.dot(dec_t[...], total.astype(BF16), preferred_element_type=F32)
        hid[rp, q - 1] = hidden
        field[layers - 1, rp, rows_of(q), :] = hidden.astype(BF16)

    def conv_at(layer, rp, q):
        window = field[layer, rp, pl.ds(pl.multiple_of((q - 1) * width, width), 3 * width), :]
        back = jnp.dot(taps[layer], window, preferred_element_type=F32)
        lon = 4 * (q - 1) + 2 * rp
        parts = []
        for r in range(2):
            lats = slice(r * tile_lat, (r + 1) * tile_lat)
            factor = gate[layer, pl.ds(lon + r, width, stride=tile_lon), :]
            parts.append(hid[rp, q - 1, :, lats] + factor * back[:, lats])
        return jnp.concatenate(parts, axis=1)

    def step(layer, rp, q):
        hidden = conv_at(layer, rp, q)
        hid[rp, q - 1] = hidden
        field[layer - 1, rp, rows_of(q), :] = hidden.astype(BF16)

    def edges_then_inside(visit, layer):
        for rp in range(2):
            visit(rp, 1)
            visit(rp, quads)
            for copy in halos(layer, rp):
                copy.start()

        @pl.loop(2, quads)
        def _(q):
            for rp in range(2):
                visit(rp, q)

    edges_then_inside(scatter, layers - 1)
    for layer in reversed(range(1, layers)):
        for rp in range(2):
            for copy in halos(layer, rp):
                copy.wait_recv()
        edges_then_inside(functools.partial(step, layer), layer - 1)

    def finish(pair):
        rows = done.at[pair].reshape(lev * 8, tile_lat)
        for half in range(2):
            for rp in range(2):
                q = 2 * pair + half + 1
                hidden = conv_at(0, rp, q).astype(BF16)
                state = cg[rp, q - 1] + jnp.dot(enc_t[...], hidden, preferred_element_type=F32)
                for r in range(2):
                    rows[pl.ds(half * 4 + rp * 2 + r, lev, stride=8), :] = state[
                        :, r * tile_lat : (r + 1) * tile_lat
                    ]
        write(pair).start()

    def write(pair):
        return pltpu.make_async_copy(
            done.at[pair, 0:levels],
            out.at[:, pl.ds(pl.multiple_of(pair * 8, 8), 8), :],
            out_sem.at[pair],
        )

    pairs = quads // 2
    pl.loop(1, pairs - 1)(finish)
    for rp in range(2):
        for copy in halos(0, rp):
            copy.wait_recv()
    finish(0)
    finish(pairs - 1)

    @pl.loop(1, devices)
    def _(off):
        slots_to(lax.rem(me + off, devices)).wait_send()

    for layer in range(layers):
        for rp in range(2):
            for copy in halos(layer, rp):
                copy.wait_send()

    @pl.loop(0, pairs)
    def _(pair):
        write(pair).wait()


def per_device(
    observation_residual, obs_index, obs_count, obs_weight, jacobian, decoder, conv_weight, gates, encoder
):
    lat_n, lon_n = lax.axis_size("lat"), lax.axis_size("lon")
    devices = lat_n * lon_n
    channels, slots = observation_residual.shape
    slot = slots // devices
    kinds_n, levels = jacobian.shape[1:]
    layers, width, tile_lon, tile_lat = gates.shape
    lev = up(levels + 2, 16)
    lanes = up(levels + 2, 128)
    quads = tile_lon // 4

    blocks = jnp.transpose(jacobian, (1, 0, 2)).reshape(kinds_n * channels, levels)
    jac = jnp.pad(blocks, ((0, 16), (0, lanes - levels)))
    row = lax.broadcasted_iota(jnp.int32, jac.shape, 0) - kinds_n * channels
    lane = lax.broadcasted_iota(jnp.int32, jac.shape, 1) - levels
    jac = jnp.where((row >= 0) & (row < 2) & (row == lane), jnp.ones((), BF16), jac)

    dims = (lat_n, lon_n, slot, kinds_n, levels, layers, width, tile_lon, tile_lat)
    vmem = pl.BlockSpec(memory_space=pltpu.VMEM)
    hbm = pl.BlockSpec(memory_space=pl.ANY)
    dma = pltpu.SemaphoreType.DMA
    return pl.pallas_call(
        functools.partial(kernel, dims),
        out_shape=jax.ShapeDtypeStruct((levels, tile_lon, tile_lat), F32),
        in_specs=[vmem] * 8 + [hbm],
        out_specs=hbm,
        scratch_shapes=[
            pltpu.VMEM((slots, lanes), BF16),
            pltpu.VMEM((slots, lanes), BF16),
            pltpu.VMEM((lev, slots), BF16),
            pltpu.VMEM((slots, tile_lat), BF16),
            pltpu.VMEM((2, quads, lev, 2 * tile_lat), F32),
            pltpu.VMEM((2, quads, width, 2 * tile_lat), F32),
            pltpu.VMEM((layers, 2, (quads + 2) * width, 2 * tile_lat), BF16),
            pltpu.VMEM((2, width, tile_lon, tile_lat), BF16),
            pltpu.VMEM((layers, width * tile_lon, tile_lat), F32),
            pltpu.VMEM((layers, width, 3 * width), BF16),
            pltpu.VMEM((width, lev), BF16),
            pltpu.VMEM((lev, width), BF16),
            pltpu.VMEM((lanes, width), F32),
            pltpu.VMEM((width, lanes), F32),
            pltpu.VMEM((quads // 2, lev, 8, tile_lat), F32),
            dma((devices,)),
            dma((devices,)),
            dma((layers, 2, 2)),
            dma((layers, 2, 2)),
            dma((2,)),
            dma((quads // 2,)),
        ],
        compiler_params=pltpu.CompilerParams(
            collective_id=0, has_side_effects=True, vmem_limit_bytes=60 * 1024 * 1024
        ),
    )(
        observation_residual, obs_index, obs_count, obs_weight.reshape(1, channels), jac,
        decoder, conv_weight, encoder, gates,
    )


def solution(mesh):
    return jax.shard_map(
        per_device,
        mesh=mesh,
        in_specs=(
            P(None, ("lat", "lon")),
            P(None, ("lat", "lon")),
            P(None, ("lat", "lon")),
            P(),
            P(),
            P(),
            P(),
            P(None, None, "lon", "lat"),
            P(),
        ),
        out_specs=P(None, "lon", "lat"),
        check_vma=False,
    )
```

time: 148 us -> 66.4 us (0.45)
  Pallas kernels: 0 us -> 56.9 us
  matrix products: 34.3 us -> 0 us
  local copies, waits for them, and re-layouts: 41.4 us -> 7.73 us
  waiting for transfers between devices: 30.2 us -> 0 us
  starting transfers between devices: 28.2 us -> 0 us
  other arithmetic: 12.6 us -> 1.54 us
    pallas_call x0 -> x1, Pallas kernels: none -> 56.9 us  [per_device(): pl.pallas_call(functools.partial(kernel, dims), out_shape=jax.ShapeDtypeS...]
    dot_general x15 -> x0, matrix products: 34.3 us -> none  [the longest x11 15.3 us: per_device(): lax.dot_general(conv_weight[layer, tap], window, (((0,), (0,)), ((), ()))...]
    convert_element_type x5 -> x0, local copies, waits for them, and re-layouts: 22.6 us -> none  [the longest x4 21.8 us: per_device(): hidden = hidden + gates[layer].reshape(width, cell_total) * back]
    ppermute x8 -> x0, waiting for transfers between devices: 20.2 us -> none  [the longest x4 13.7 us: with_halo(): lax.ppermute(lax.slice_in_dim(block, block.shape[dim] - width, None, axis...]
    all_to_all x4 -> x0, starting transfers between devices: 17.3 us -> none  [the longest x1 6.21 us: per_device(): lax.all_to_all(lax.all_to_all(obs_index[0:1].reshape(1, lat_count, lon_co...]
    ppermute x8 -> x0, starting transfers between devices: 10.9 us -> none  [the longest x4 6.04 us: with_halo(): lax.ppermute(lax.slice_in_dim(block, block.shape[dim] - width, None, axis...]
    convert_element_type x2 -> x0, other arithmetic: 10.1 us -> none  [the longest x1 10.1 us: per_device(): hidden = hidden + gates[layer].reshape(width, cell_total) * back]
    all_to_all x4 -> x0, waiting for transfers between devices: 9.99 us -> none  [the longest x1 5.85 us: per_device(): lax.all_to_all(lax.all_to_all(obs_index[0:1].reshape(1, lat_count, lon_co...]
  transfers between devices with their start and end apart: 12 -> 0, of which waited for: 10 -> 0; matrix products, arithmetic and copies ran while one was open for 32% -> 0% of each run, Pallas kernels for 0% -> 0%
where the time goes in v1:
time: 66.4 us; the launch traced here: 66.1 us
  Pallas kernels  56.9 us (86%)
  local copies, waits for them, and re-layouts  7.73 us (12%)
  other arithmetic  1.54 us (2%)
    pallas_call x1, Pallas kernels, per_device(): pl.pallas_call(functools.partial(kernel, dims), out_shape=jax.ShapeDtypeS...  56.9 us
    unnamed x2, local copies, waits for them, and re-layouts  6.54 us
    select_n x1, other arithmetic, per_device(): jnp.where((row >= 0) & (row < 2) & (row == lane), jnp.ones((), BF16), jac)  1.52 us

profile of v1, /device:TPU:0, one launch (start us, length us, event | category | flops | bytes accessed | tf_op | source)
XLA Modules:
  0.0 66.1 jit_solution(14779769775074958343)
XLA Ops:
  0.0 1.5 %copy.11.enc = bf16[128,137]{1,0:T(8,128)(2,1)} copy(bf16[128,137]{0,1:T(8,128)(2,1)} %param.17) | data formatting | bytes 70144 | tf_op args[8]
  1.5 1.2 %copy.10 = bf16[8,128,137]{2,1,0:T(8,128)(2,1)S(1)} copy(bf16[8,128,137]{1,0,2:T(8,128)(2,1)} %bitcast.4) | data formatting | bytes 561152 | tf_op jit(solution)/shard_map/transpose | solution.py:269
  2.7 1.5 %and_select_fusion.jac = bf16[1040,256]{1,0:T(8,128)(2,1)} fusion(bf16[1024,137]{1,0:T(8,128)(2,1)S(1)} %bitcast.3, s32[256]{0:T(256)S(1)} %iota_add_fusion.1, s32[1040]{0:T(1024)S(1)} %iota_add_fusion, pred[1040]{0:T(1024)(128)(4,1)S(1)} %compare_and_fusion), kind=kLoop, calls=%fused_computation | loop fusion | flops 798720 | bytes 819280 | tf_op jit(solution)/shard_map/jit(_where)/select_n | solution.py:273
  4.2 56.9 %shard_map.91 = f32[137,64,128]{2,1,0:T(8,128)} custom-call(bf16[128,512]{1,0:T(8,128)(2,1)} %resid.1, s32[2,512]{1,0:T(2,128)} %index.1, s32[1,32]{1,0:T(1,128)} %counts.1, f32[1,128]{1,0:T(1,128)} %bitcast.5, bf16[1040,256]{1,0:T(8,128)(2,1)} %and_select_fusion.jac, bf16[137,128]{1,0:T(8,128)(2,1)} %dec.1, bf16[4,3,128,128]{3,2,1,0:T(8,128)(2,1)} %conv.1, ...), custom_call_target="tpu_custom_call" | custom-call | tf_op jit(solution)/shard_map/pallas_call | solution.py:279
  61.1 5.0 %copy.13 = f32[137,64,128]{2,1,0:T(8,128)} copy(f32[137,64,128]{2,1,0:T(8,128)} %shard_map.91) | data formatting | bytes 8978432
  (3 shorter events, 0.0 us)

commit v2 on v1

--- a/solution.py
+++ b/solution.py
@@ -18,8 +18,8 @@
 
 def kernel(
     dims,
-    resid, index, counts, weight, jac, dec, conv, enc, gates, out,
-    sent, got, incr, place, cg, hid, field, stage, gate, taps, dec_t, enc_t, tall, wide, done,
+    resid, index, counts, weight, jac, dec, conv, gates, cg_out, hid_out,
+    sent, got, incr, place, cg, hid, last, field, stage, gate, taps, dec_t, tall, blocks, jac_l,
     a2a_send, a2a_recv, halo_send, halo_recv, gate_sem, out_sem,
 ):
     lat_n, lon_n, slot, kinds_n, levels, layers, width, tile_lon, tile_lat = dims
@@ -46,11 +46,43 @@
             barrier, inc=1, device_id=(d // lon_n, lax.rem(d, lon_n)), device_id_type=MESH
         )
 
+    channels = resid.shape[0]
+    blocks[...] = jnp.zeros_like(blocks)
+    blocks[0 : levels * kinds_n, :] = jac[...].astype(F32).reshape(levels * kinds_n, -1)
+    for k in range(kinds_n):
+        jac_l[:, k * channels : (k + 1) * channels] = blocks[pl.ds(k, lev, stride=kinds_n), :].astype(BF16)
     weight_lanes = jnp.transpose(jnp.broadcast_to(weight[...], (128, weight.shape[1])))
     counts8 = jnp.broadcast_to(counts[...].astype(F32), (8, devices)).astype(BF16)
-
-    @pl.loop(0, devices * slot // 128)
-    def _(chunk):
+    mine = pl.ds(pl.multiple_of(me * slot, slot), slot)
+
+    def slots_to(d):
+        return pltpu.make_async_remote_copy(
+            src_ref=sent.at[pl.ds(pl.multiple_of(d * slot, slot), slot)],
+            dst_ref=got.at[mine],
+            send_sem=a2a_send.at[d],
+            recv_sem=a2a_recv.at[me],
+            device_id=(d // lon_n, lax.rem(d, lon_n)),
+            device_id_type=MESH,
+        )
+
+    def slots_from(s):
+        return pltpu.make_async_remote_copy(
+            src_ref=sent.at[mine],
+            dst_ref=got.at[pl.ds(pl.multiple_of(s * slot, slot), slot)],
+            send_sem=a2a_send.at[s],
+            recv_sem=a2a_recv.at[s],
+            device_id=(s // lon_n, lax.rem(s, lon_n)),
+            device_id_type=MESH,
+        )
+
+    pl.semaphore_wait(barrier, devices - 1)
+
+    chunks = devices * slot // 128
+    per_chunk = 128 // slot
+
+    @pl.loop(0, chunks)
+    def _(turn):
+        chunk = lax.rem(turn + me // per_chunk + 1, chunks)
         lanes = pl.ds(pl.multiple_of(chunk * 128, 128), 128)
         pair = (lax.broadcasted_iota(jnp.int32, (devices, 128), 1) + chunk * 128) // slot
         owner = lax.broadcasted_iota(jnp.int32, (devices, 128), 0)
@@ -61,45 +93,24 @@
         weighted = jnp.where(used, weight_lanes * resid[:, lanes].astype(F32), 0.0)
         kinds = index[1:2, lanes]
         cells = index[0:1, lanes]
-        rows = [
-            jnp.where(kinds == k, weighted, 0.0).astype(BF16) for k in range(kinds_n)
-        ]
-        row = lax.broadcasted_iota(jnp.int32, (16, 128), 0)
+        stack = jnp.concatenate(
+            [jnp.where(kinds == k, weighted, 0.0).astype(BF16) for k in range(kinds_n)], axis=0
+        )
+        value = jnp.dot(jac_l[...], stack, preferred_element_type=F32)
+        row = lax.broadcasted_iota(jnp.int32, (lev, 128), 0)
         lon = (cells // tile_lat).astype(F32)
         lat = (cells % tile_lat).astype(F32)
-        rows.append(jnp.where(row == 0, lon, jnp.where(row == 1, lat, 0.0)).astype(BF16))
-        stack = jnp.concatenate(rows, axis=0)
-        sent[lanes, :] = lax.dot_general(
-            stack, jac[...], (((0,), (0,)), ((), ())), preferred_element_type=F32
-        ).astype(BF16)
-
-    pl.semaphore_wait(barrier, devices - 1)
-
-    mine = pl.ds(pl.multiple_of(me * slot, slot), slot)
-
-    def slots_to(d):
-        return pltpu.make_async_remote_copy(
-            src_ref=sent.at[pl.ds(pl.multiple_of(d * slot, slot), slot)],
-            dst_ref=got.at[mine],
-            send_sem=a2a_send.at[d],
-            recv_sem=a2a_recv.at[me],
-            device_id=(d // lon_n, lax.rem(d, lon_n)),
-            device_id_type=MESH,
-        )
-
-    def slots_from(s):
-        return pltpu.make_async_remote_copy(
-            src_ref=sent.at[mine],
-            dst_ref=got.at[pl.ds(pl.multiple_of(s * slot, slot), slot)],
-            send_sem=a2a_send.at[s],
-            recv_sem=a2a_recv.at[s],
-            device_id=(s // lon_n, lax.rem(s, lon_n)),
-            device_id_type=MESH,
-        )
-
-    @pl.loop(1, devices)
-    def _(off):
-        slots_to(lax.rem(me + off, devices)).start()
+        value = jnp.where(row == levels, lon, jnp.where(row == levels + 1, lat, value))
+        pad = jnp.zeros((sent.shape[1] - lev, 128), F32)
+        sent[lanes, :] = jnp.transpose(jnp.concatenate([value, pad], axis=0)).astype(BF16)
+
+        @pl.loop(0, per_chunk)
+        def _(nth):
+            d = chunk * per_chunk + lax.rem(nth + me, per_chunk)
+
+            @pl.when(d != me)
+            def _():
+                slots_to(d).start()
 
     got[mine, :] = sent[mine, :]
 
@@ -111,9 +122,6 @@
     tall[...] = jnp.zeros_like(tall)
     tall[0:levels, :] = dec[...].astype(F32)
     dec_t[...] = jnp.transpose(tall[...])[:, 0:lev].astype(BF16)
-    wide[...] = jnp.zeros_like(wide)
-    wide[:, 0:levels] = enc[...].astype(F32)
-    enc_t[...] = jnp.transpose(wide[...])[0:lev].astype(BF16)
 
     for at, layer in enumerate(order):
         gate_copy(layer).wait()
@@ -171,8 +179,9 @@
             value = jnp.full((1, tile_lat), lon + r, jnp.int32).astype(F32).astype(BF16)
             hot.append(jnp.where(place[...] == value, 1.0, 0.0).astype(BF16))
         total = jnp.dot(incr[...], jnp.concatenate(hot, axis=1), preferred_element_type=F32)
-        cg[rp, q - 1] = total
-        hidden = jnp.dot(dec_t[...], total.astype(BF16), preferred_element_type=F32)
+        narrow = total.astype(BF16)
+        cg[rp, q - 1] = narrow
+        hidden = jnp.dot(dec_t[...], narrow, preferred_element_type=F32)
         hid[rp, q - 1] = hidden
         field[layers - 1, rp, rows_of(q), :] = hidden.astype(BF16)
 
@@ -205,39 +214,31 @@
                 visit(rp, q)
 
     edges_then_inside(scatter, layers - 1)
+    cg_copy = pltpu.make_async_copy(cg, cg_out, out_sem.at[0])
+    cg_copy.start()
     for layer in reversed(range(1, layers)):
         for rp in range(2):
             for copy in halos(layer, rp):
                 copy.wait_recv()
         edges_then_inside(functools.partial(step, layer), layer - 1)
 
-    def finish(pair):
-        rows = done.at[pair].reshape(lev * 8, tile_lat)
-        for half in range(2):
-            for rp in range(2):
-                q = 2 * pair + half + 1
-                hidden = conv_at(0, rp, q).astype(BF16)
-                state = cg[rp, q - 1] + jnp.dot(enc_t[...], hidden, preferred_element_type=F32)
-                for r in range(2):
-                    rows[pl.ds(half * 4 + rp * 2 + r, lev, stride=8), :] = state[
-                        :, r * tile_lat : (r + 1) * tile_lat
-                    ]
-        write(pair).start()
-
-    def write(pair):
-        return pltpu.make_async_copy(
-            done.at[pair, 0:levels],
-            out.at[:, pl.ds(pl.multiple_of(pair * 8, 8), 8), :],
-            out_sem.at[pair],
-        )
-
-    pairs = quads // 2
-    pl.loop(1, pairs - 1)(finish)
+    def finish(q):
+        for rp in range(2):
+            last[rp, q - 1] = conv_at(0, rp, q).astype(BF16)
+
+    def hid_copy(start, count, sem):
+        part = pl.ds(start, count)
+        return pltpu.make_async_copy(last.at[:, part], hid_out.at[:, part], out_sem.at[sem])
+
+    pl.loop(2, quads)(finish)
+    hid_copy(1, quads - 2, 1).start()
     for rp in range(2):
         for copy in halos(0, rp):
             copy.wait_recv()
-    finish(0)
-    finish(pairs - 1)
+    finish(1)
+    hid_copy(0, 1, 2).start()
+    finish(quads)
+    hid_copy(quads - 1, 1, 3).start()
 
     @pl.loop(1, devices)
     def _(off):
@@ -248,9 +249,24 @@
             for copy in halos(layer, rp):
                 copy.wait_send()
 
-    @pl.loop(0, pairs)
-    def _(pair):
-        write(pair).wait()
+    cg_copy.wait()
+    hid_copy(1, quads - 2, 1).wait()
+    hid_copy(0, 1, 2).wait()
+    hid_copy(quads - 1, 1, 3).wait()
+
+
+def encode_kernel(cg, hid, enc, out):
+    levels, lons, tile_lat = out.shape
+    rows = out.reshape(levels * lons, tile_lat)
+    for half in range(2):
+        for rp in range(2):
+            state = cg[rp, half, 0:levels].astype(F32) + jnp.dot(
+                enc[...], hid[rp, half], preferred_element_type=F32
+            )
+            for r in range(2):
+                rows[pl.ds(half * 4 + rp * 2 + r, levels, stride=lons), :] = state[
+                    :, r * tile_lat : (r + 1) * tile_lat
+                ]
 
 
 def per_device(
@@ -266,51 +282,62 @@
     lanes = up(levels + 2, 128)
     quads = tile_lon // 4
 
-    blocks = jnp.transpose(jacobian, (1, 0, 2)).reshape(kinds_n * channels, levels)
-    jac = jnp.pad(blocks, ((0, 16), (0, lanes - levels)))
-    row = lax.broadcasted_iota(jnp.int32, jac.shape, 0) - kinds_n * channels
-    lane = lax.broadcasted_iota(jnp.int32, jac.shape, 1) - levels
-    jac = jnp.where((row >= 0) & (row < 2) & (row == lane), jnp.ones((), BF16), jac)
-
     dims = (lat_n, lon_n, slot, kinds_n, levels, layers, width, tile_lon, tile_lat)
     vmem = pl.BlockSpec(memory_space=pltpu.VMEM)
     hbm = pl.BlockSpec(memory_space=pl.ANY)
     dma = pltpu.SemaphoreType.DMA
-    return pl.pallas_call(
+    cg_shape = (2, quads, lev, 2 * tile_lat)
+    hid_shape = (2, quads, width, 2 * tile_lat)
+    column_grad, hidden = pl.pallas_call(
         functools.partial(kernel, dims),
-        out_shape=jax.ShapeDtypeStruct((levels, tile_lon, tile_lat), F32),
-        in_specs=[vmem] * 8 + [hbm],
-        out_specs=hbm,
+        out_shape=[
+            jax.ShapeDtypeStruct(cg_shape, BF16),
+            jax.ShapeDtypeStruct(hid_shape, BF16),
+        ],
+        in_specs=[vmem] * 7 + [hbm],
+        out_specs=[hbm, hbm],
         scratch_shapes=[
             pltpu.VMEM((slots, lanes), BF16),
             pltpu.VMEM((slots, lanes), BF16),
             pltpu.VMEM((lev, slots), BF16),
             pltpu.VMEM((slots, tile_lat), BF16),
-            pltpu.VMEM((2, quads, lev, 2 * tile_lat), F32),
-            pltpu.VMEM((2, quads, width, 2 * tile_lat), F32),
+            pltpu.VMEM(cg_shape, BF16),
+            pltpu.VMEM(hid_shape, F32),
+            pltpu.VMEM(hid_shape, BF16),
             pltpu.VMEM((layers, 2, (quads + 2) * width, 2 * tile_lat), BF16),
             pltpu.VMEM((2, width, tile_lon, tile_lat), BF16),
             pltpu.VMEM((layers, width * tile_lon, tile_lat), F32),
             pltpu.VMEM((layers, width, 3 * width), BF16),
             pltpu.VMEM((width, lev), BF16),
-            pltpu.VMEM((lev, width), BF16),
             pltpu.VMEM((lanes, width), F32),
-            pltpu.VMEM((width, lanes), F32),
-            pltpu.VMEM((quads // 2, lev, 8, tile_lat), F32),
+            pltpu.VMEM((lev * kinds_n, channels), F32),
+            pltpu.VMEM((lev, kinds_n * channels), BF16),
             dma((devices,)),
             dma((devices,)),
             dma((layers, 2, 2)),
             dma((layers, 2, 2)),
             dma((2,)),
-            dma((quads // 2,)),
+            dma((4,)),
         ],
         compiler_params=pltpu.CompilerParams(
             collective_id=0, has_side_effects=True, vmem_limit_bytes=60 * 1024 * 1024
         ),
     )(
-        observation_residual, obs_index, obs_count, obs_weight.reshape(1, channels), jac,
-        decoder, conv_weight, encoder, gates,
+        observation_residual, obs_index, obs_count, obs_weight.reshape(1, channels),
+        jnp.transpose(jacobian, (2, 1, 0)), decoder, conv_weight, gates,
     )
+    return pl.pallas_call(
+        encode_kernel,
+        out_shape=jax.ShapeDtypeStruct((levels, tile_lon, tile_lat), F32),
+        grid=(quads // 2,),
+        in_specs=[
+            pl.BlockSpec((2, 2, lev, 2 * tile_lat), lambda p: (0, p, 0, 0)),
+            pl.BlockSpec((2, 2, width, 2 * tile_lat), lambda p: (0, p, 0, 0)),
+            pl.BlockSpec((levels, width), lambda p: (0, 0)),
+        ],
+        out_specs=pl.BlockSpec((levels, 8, tile_lat), lambda p: (0, p, 0)),
+        compiler_params=pltpu.CompilerParams(vmem_limit_bytes=32 * 1024 * 1024),
+    )(column_grad, hidden, jnp.transpose(encoder))
 
 
 def solution(mesh):

time: 66.4 us -> 62.8 us (0.946)
  local copies, waits for them, and re-layouts: 7.73 us -> 3.25 us
  Pallas kernels: 56.9 us -> 59.3 us
  other arithmetic: 1.54 us -> 0 us
    unnamed x2 -> x6, local copies, waits for them, and re-layouts: 6.54 us -> 3.25 us
    pallas_call x1 -> x2, Pallas kernels: 56.9 us -> 59.3 us  [the longest x1 54.7 us: per_device(): pl.pallas_call(functools.partial(kernel, dims), out_shape=[jax.ShapeDtype...]
    select_n x1 -> x0, other arithmetic: 1.52 us -> none  [per_device(): jnp.where((row >= 0) & (row < 2) & (row == lane), jnp.ones((), BF16), jac)]
    transpose x1 -> x0, local copies, waits for them, and re-layouts: 1.19 us -> none  [per_device(): jnp.transpose(jacobian, (1, 0, 2)).reshape(kinds_n * channels, levels)]
where the time goes in v2:
time: 62.8 us; the launch traced here: 62.6 us
  Pallas kernels  59.3 us (94%)
  local copies, waits for them, and re-layouts  3.25 us (5%)
    pallas_call x1, Pallas kernels, per_device(): pl.pallas_call(functools.partial(kernel, dims), out_shape=[jax.ShapeDtype...  54.7 us
    pallas_call x1, Pallas kernels, per_device(): pl.pallas_call(encode_kernel, out_shape=jax.ShapeDtypeStruct((levels, til...  4.64 us
    unnamed x6, local copies, waits for them, and re-layouts  3.25 us

profile of v2, /device:TPU:0, one launch (start us, length us, event | category | flops | bytes accessed | tf_op | source)
XLA Modules:
  0.0 62.6 jit_solution(13430319331283182809)
XLA Ops:
  0.0 0.0 copy-start.2
  0.0 54.7 %shard_map.91 = (bf16[2,16,144,256]{3,2,1,0:T(8,128)(2,1)}, bf16[2,16,128,256]{3,2,1,0:T(8,128)(2,1)}) custom-call(bf16[128,512]{1,0:T(8,128)(2,1)} %resid.1, s32[2,512]{1,0:T(2,128)} %index.1, s32[1,32]{1,0:T(1,128)} %counts.1, f32[1,128]{1,0:T(1,128)} %bitcast.5, bf16[137,8,128]{2,1,0:T(8,128)(2,1)} %bitcast.4, bf16[137,128]{1,0:T(8,128)(2,1)} %dec.1, ...), custom_call_target="tpu_custom_call" | custom-call | tf_op jit(solution)/shard_map/pallas_call | solution.py:291
  54.7 0.0 copy-done.2
  54.7 0.0 copy-start
  54.7 1.7 %copy-done = bf16[2,16,144,256]{3,2,1,0:T(8,128)(2,1)S(1)} copy-done((bf16[2,16,144,256]{3,2,1,0:T(8,128)(2,1)S(1)}, bf16[2,16,144,256]{3,2,1,0:T(8,128)(2,1)}, u32[]{:S(2)}) %copy-start) | copy-done | bytes 2359320
  56.4 0.0 copy-start.1
  56.4 1.6 %copy-done.1 = bf16[2,16,128,256]{3,2,1,0:T(8,128)(2,1)S(1)} copy-done((bf16[2,16,128,256]{3,2,1,0:T(8,128)(2,1)S(1)}, bf16[2,16,128,256]{3,2,1,0:T(8,128)(2,1)}, u32[]{:S(2)}) %copy-start.1) | copy-done | bytes 2097176
  58.0 4.6 %shard_map.92 = f32[137,64,128]{2,1,0:T(8,128)} custom-call(bf16[2,16,144,256]{3,2,1,0:T(8,128)(2,1)S(1)} %copy-done, bf16[2,16,128,256]{3,2,1,0:T(8,128)(2,1)S(1)} %copy-done.1, bf16[137,128]{1,0:T(8,128)(2,1)S(1)} %bitcast.3), custom_call_target="tpu_custom_call" | custom-call | tf_op jit(solution)/shard_map/pallas_call | solution.py:329
Async XLA Ops:
  0.0 54.7 %copy-start.2 = (bf16[128,137]{0,1:T(8,128)(2,1)S(1)}, bf16[128,137]{0,1:T(8,128)(2,1)}, u32[]{:S(2)}) copy-start(bf16[128,137]{0,1:T(8,128)(2,1)} %param.17) | copy-start | bytes 105220
  54.7 1.7 %copy-start = (bf16[2,16,144,256]{3,2,1,0:T(8,128)(2,1)S(1)}, bf16[2,16,144,256]{3,2,1,0:T(8,128)(2,1)}, u32[]{:S(2)}) copy-start(bf16[2,16,144,256]{3,2,1,0:T(8,128)(2,1)} %get-tuple-element.7.cg) | copy-start | bytes 7077892
  56.4 1.6 %copy-start.1 = (bf16[2,16,128,256]{3,2,1,0:T(8,128)(2,1)S(1)}, bf16[2,16,128,256]{3,2,1,0:T(8,128)(2,1)}, u32[]{:S(2)}) copy-start(bf16[2,16,128,256]{3,2,1,0:T(8,128)(2,1)} %get-tuple-element.8.hid) | copy-start | bytes 6291460

commit v3 on v2

--- a/solution.py
+++ b/solution.py
@@ -14,6 +14,10 @@
 
 def up(value, unit):
     return (value + unit - 1) // unit * unit
+
+
+def odd(rows):
+    return rows // 2 * 2 + 1
 
 
 def kernel(
@@ -26,6 +30,7 @@
     devices = lat_n * lon_n
     lev = incr.shape[0]
     quads = tile_lon // 4
+    pitch = odd(tile_lon)
     my_lat, my_lon = lax.axis_index("lat"), lax.axis_index("lon")
     me = my_lat * lon_n + my_lon
     right, left = lax.rem(my_lon + 1, lon_n), lax.rem(my_lon + lon_n - 1, lon_n)
@@ -130,8 +135,7 @@
         def _(block):
             for part in range(4):
                 c = block * 4 + part
-                rows = pl.ds(pl.multiple_of(c * tile_lon, tile_lon), tile_lon)
-                gate[layer, rows, :] = stage[layer % 2, c].astype(F32)
+                gate[layer, pl.ds(c * pitch, tile_lon), :] = stage[layer % 2, c].astype(F32)
 
         if at + 2 < layers:
             gate_copy(order[at + 2]).start()
@@ -192,7 +196,7 @@
         parts = []
         for r in range(2):
             lats = slice(r * tile_lat, (r + 1) * tile_lat)
-            factor = gate[layer, pl.ds(lon + r, width, stride=tile_lon), :]
+            factor = gate[layer, pl.ds(lon + r, width, stride=pitch), :]
             parts.append(hid[rp, q - 1, :, lats] + factor * back[:, lats])
         return jnp.concatenate(parts, axis=1)
 
@@ -255,18 +259,21 @@
     hid_copy(quads - 1, 1, 3).wait()
 
 
-def encode_kernel(cg, hid, enc, out):
+def encode_kernel(cg, hid, enc, out, slabs):
     levels, lons, tile_lat = out.shape
-    rows = out.reshape(levels * lons, tile_lat)
+    pitch = odd(levels)
     for half in range(2):
         for rp in range(2):
             state = cg[rp, half, 0:levels].astype(F32) + jnp.dot(
                 enc[...], hid[rp, half], preferred_element_type=F32
             )
             for r in range(2):
-                rows[pl.ds(half * 4 + rp * 2 + r, levels, stride=lons), :] = state[
+                lon = half * 4 + rp * 2 + r
+                slabs[lon * pitch : lon * pitch + levels, :] = state[
                     :, r * tile_lat : (r + 1) * tile_lat
                 ]
+    for level in range(levels):
+        out[level] = slabs[pl.ds(level, lons, stride=pitch), :]
 
 
 def per_device(
@@ -306,7 +313,7 @@
             pltpu.VMEM(hid_shape, BF16),
             pltpu.VMEM((layers, 2, (quads + 2) * width, 2 * tile_lat), BF16),
             pltpu.VMEM((2, width, tile_lon, tile_lat), BF16),
-            pltpu.VMEM((layers, width * tile_lon, tile_lat), F32),
+            pltpu.VMEM((layers, up(width * odd(tile_lon), 8), tile_lat), F32),
             pltpu.VMEM((layers, width, 3 * width), BF16),
             pltpu.VMEM((width, lev), BF16),
             pltpu.VMEM((lanes, width), F32),
@@ -336,7 +343,8 @@
             pl.BlockSpec((levels, width), lambda p: (0, 0)),
         ],
         out_specs=pl.BlockSpec((levels, 8, tile_lat), lambda p: (0, p, 0)),
-        compiler_params=pltpu.CompilerParams(vmem_limit_bytes=32 * 1024 * 1024),
+        scratch_shapes=[pltpu.VMEM((up(8 * odd(levels), 8), tile_lat), F32)],
+        compiler_params=pltpu.CompilerParams(vmem_limit_bytes=60 * 1024 * 1024),
     )(column_grad, hidden, jnp.transpose(encoder))
 
 

time: 62.8 us -> 61.1 us (0.973)
  local copies, waits for them, and re-layouts: 3.25 us -> 0 us
  Pallas kernels: 59.3 us -> 60.7 us
    unnamed x6 -> x0, local copies, waits for them, and re-layouts: 3.25 us -> none
    pallas_call x1, Pallas kernels: 4.64 us -> 7.53 us  [per_device(): pl.pallas_call(encode_kernel, out_shape=jax.ShapeDtypeStruct((levels, til...]
    pallas_call x1, Pallas kernels: 54.7 us -> 53.2 us  [per_device(): pl.pallas_call(functools.partial(kernel, dims), out_shape=[jax.ShapeDtype...]
where the time goes in v3:
time: 61.1 us; the launch traced here: 60.8 us
  Pallas kernels  60.7 us (99%)
    pallas_call x1, Pallas kernels, per_device(): pl.pallas_call(functools.partial(kernel, dims), out_shape=[jax.ShapeDtype...  53.2 us
    pallas_call x1, Pallas kernels, per_device(): pl.pallas_call(encode_kernel, out_shape=jax.ShapeDtypeStruct((levels, til...  7.53 us

profile of v3, /device:TPU:0, one launch (start us, length us, event | category | flops | bytes accessed | tf_op | source)
XLA Modules:
  0.0 60.8 jit_solution(9072307795900611260)
XLA Ops:
  0.0 53.2 %shard_map.91 = (bf16[2,16,144,256]{3,2,1,0:T(8,128)(2,1)}, bf16[2,16,128,256]{3,2,1,0:T(8,128)(2,1)}) custom-call(bf16[128,512]{1,0:T(8,128)(2,1)} %resid.1, s32[2,512]{1,0:T(2,128)} %index.1, s32[1,32]{1,0:T(1,128)} %counts.1, f32[1,128]{1,0:T(1,128)} %bitcast.5, bf16[137,8,128]{2,1,0:T(8,128)(2,1)} %bitcast.3, bf16[137,128]{1,0:T(8,128)(2,1)} %dec.1, ...), custom_call_target="tpu_custom_call" | custom-call | tf_op jit(solution)/shard_map/pallas_call | solution.py:298
  53.2 7.5 %shard_map.92 = f32[137,64,128]{2,1,0:T(8,128)} custom-call(bf16[2,16,144,256]{3,2,1,0:T(8,128)(2,1)} %get-tuple-element.7.cg, bf16[2,16,128,256]{3,2,1,0:T(8,128)(2,1)} %get-tuple-element.8.hid, bf16[137,128]{1,0:T(8,128)(2,1)} %bitcast.4), custom_call_target="tpu_custom_call" | custom-call | tf_op jit(solution)/shard_map/pallas_call | solution.py:336

commit v4 on v3

--- a/solution.py
+++ b/solution.py
@@ -128,7 +128,7 @@
     tall[0:levels, :] = dec[...].astype(F32)
     dec_t[...] = jnp.transpose(tall[...])[:, 0:lev].astype(BF16)
 
-    for at, layer in enumerate(order):
+    def open_gate(layer):
         gate_copy(layer).wait()
 
         @pl.loop(0, width // 4)
@@ -137,8 +137,8 @@
                 c = block * 4 + part
                 gate[layer, pl.ds(c * pitch, tile_lon), :] = stage[layer % 2, c].astype(F32)
 
-        if at + 2 < layers:
-            gate_copy(order[at + 2]).start()
+        if layer >= 2:
+            gate_copy(layer - 2).start()
 
     @pl.loop(1, devices)
     def _(off):
@@ -221,6 +221,7 @@
     cg_copy = pltpu.make_async_copy(cg, cg_out, out_sem.at[0])
     cg_copy.start()
     for layer in reversed(range(1, layers)):
+        open_gate(layer)
         for rp in range(2):
             for copy in halos(layer, rp):
                 copy.wait_recv()
@@ -234,6 +235,7 @@
         part = pl.ds(start, count)
         return pltpu.make_async_copy(last.at[:, part], hid_out.at[:, part], out_sem.at[sem])
 
+    open_gate(0)
     pl.loop(2, quads)(finish)
     hid_copy(1, quads - 2, 1).start()
     for rp in range(2):
@@ -259,21 +261,48 @@
     hid_copy(quads - 1, 1, 3).wait()
 
 
-def encode_kernel(cg, hid, enc, out, slabs):
-    levels, lons, tile_lat = out.shape
+def encode_kernel(cg_in, hid_in, enc, out, cg, hid, slabs, done, in_sem, out_sem):
+    pairs, levels, lons, tile_lat = done.shape
     pitch = odd(levels)
-    for half in range(2):
-        for rp in range(2):
-            state = cg[rp, half, 0:levels].astype(F32) + jnp.dot(
-                enc[...], hid[rp, half], preferred_element_type=F32
-            )
-            for r in range(2):
-                lon = half * 4 + rp * 2 + r
-                slabs[lon * pitch : lon * pitch + levels, :] = state[
-                    :, r * tile_lat : (r + 1) * tile_lat
-                ]
-    for level in range(levels):
-        out[level] = slabs[pl.ds(level, lons, stride=pitch), :]
+
+    def reads(pair):
+        part = pl.ds(2 * pair, 2)
+        return (
+            pltpu.make_async_copy(cg_in.at[:, part], cg.at[:, part], in_sem.at[pair, 0]),
+            pltpu.make_async_copy(hid_in.at[:, part], hid.at[:, part], in_sem.at[pair, 1]),
+        )
+
+    def write(pair):
+        part = pl.ds(pl.multiple_of(lons * pair, lons), lons)
+        return pltpu.make_async_copy(done.at[pair], out.at[:, part, :], out_sem.at[pair])
+
+    @pl.loop(0, pairs)
+    def _(pair):
+        for copy in reads(pair):
+            copy.start()
+
+    @pl.loop(0, pairs)
+    def _(pair):
+        for copy in reads(pair):
+            copy.wait()
+        for half in range(2):
+            for rp in range(2):
+                q = 2 * pair + half
+                state = cg[rp, q, 0:levels].astype(F32) + jnp.dot(
+                    enc[...], hid[rp, q], preferred_element_type=F32
+                )
+                for r in range(2):
+                    lon = half * 4 + rp * 2 + r
+                    slabs[lon * pitch : lon * pitch + levels, :] = state[
+                        :, r * tile_lat : (r + 1) * tile_lat
+                    ]
+        for level in range(levels):
+            done[pair, level] = slabs[pl.ds(level, lons, stride=pitch), :]
+        write(pair).start()
+
+    @pl.loop(0, pairs)
+    def _(pair):
+        write(pair).wait()
 
 
 def per_device(
@@ -336,14 +365,16 @@
     return pl.pallas_call(
         encode_kernel,
         out_shape=jax.ShapeDtypeStruct((levels, tile_lon, tile_lat), F32),
-        grid=(quads // 2,),
-        in_specs=[
-            pl.BlockSpec((2, 2, lev, 2 * tile_lat), lambda p: (0, p, 0, 0)),
-            pl.BlockSpec((2, 2, width, 2 * tile_lat), lambda p: (0, p, 0, 0)),
-            pl.BlockSpec((levels, width), lambda p: (0, 0)),
+        in_specs=[hbm, hbm, vmem],
+        out_specs=hbm,
+        scratch_shapes=[
+            pltpu.VMEM(cg_shape, BF16),
+            pltpu.VMEM(hid_shape, BF16),
+            pltpu.VMEM((up(8 * odd(levels), 8), tile_lat), F32),
+            pltpu.VMEM((quads // 2, levels, 8, tile_lat), F32),
+            dma((quads // 2, 2)),
+            dma((quads // 2,)),
         ],
-        out_specs=pl.BlockSpec((levels, 8, tile_lat), lambda p: (0, p, 0)),
-        scratch_shapes=[pltpu.VMEM((up(8 * odd(levels), 8), tile_lat), F32)],
         compiler_params=pltpu.CompilerParams(vmem_limit_bytes=60 * 1024 * 1024),
     )(column_grad, hidden, jnp.transpose(encoder))
 

time: 61.1 us -> 59.4 us (0.972)
  Pallas kernels: 60.7 us -> 59.2 us
    pallas_call x1, Pallas kernels: 7.53 us -> 4.96 us  [per_device(): pl.pallas_call(encode_kernel, out_shape=jax.ShapeDtypeStruct((levels, til...]
    pallas_call x1, Pallas kernels: 53.2 us -> 54.2 us  [per_device(): pl.pallas_call(functools.partial(kernel, dims), out_shape=[jax.ShapeDtype...]
where the time goes in v4:
time: 59.4 us; the launch traced here: 59.2 us
  Pallas kernels  59.2 us (100%)
    pallas_call x1, Pallas kernels, per_device(): pl.pallas_call(functools.partial(kernel, dims), out_shape=[jax.ShapeDtype...  54.2 us
    pallas_call x1, Pallas kernels, per_device(): pl.pallas_call(encode_kernel, out_shape=jax.ShapeDtypeStruct((levels, til...  4.96 us

profile of v4, /device:TPU:0, one launch (start us, length us, event | category | flops | bytes accessed | tf_op | source)
XLA Modules:
  0.0 59.2 jit_solution(8430214695088611318)
XLA Ops:
  0.0 54.2 %shard_map.91 = (bf16[2,16,144,256]{3,2,1,0:T(8,128)(2,1)}, bf16[2,16,128,256]{3,2,1,0:T(8,128)(2,1)}) custom-call(bf16[128,512]{1,0:T(8,128)(2,1)} %resid.1, s32[2,512]{1,0:T(2,128)} %index.1, s32[1,32]{1,0:T(1,128)} %counts.1, f32[1,128]{1,0:T(1,128)} %bitcast.5, bf16[137,8,128]{2,1,0:T(8,128)(2,1)} %bitcast.3, bf16[137,128]{1,0:T(8,128)(2,1)} %dec.1, ...), custom_call_target="tpu_custom_call" | custom-call | tf_op jit(solution)/shard_map/pallas_call | solution.py:327
  54.2 5.0 %shard_map.92 = f32[137,64,128]{2,1,0:T(8,128)} custom-call(bf16[2,16,144,256]{3,2,1,0:T(8,128)(2,1)} %get-tuple-element.7.cg_in, bf16[2,16,128,256]{3,2,1,0:T(8,128)(2,1)} %get-tuple-element.8.hid_in, bf16[137,128]{1,0:T(8,128)(2,1)} %bitcast.4), custom_call_target="tpu_custom_call" | custom-call | tf_op jit(solution)/shard_map/pallas_call | solution.py:365

commit v5 on v4

--- a/solution.py
+++ b/solution.py
@@ -140,6 +140,9 @@
         if layer >= 2:
             gate_copy(layer - 2).start()
 
+    for layer in order:
+        open_gate(layer)
+
     @pl.loop(1, devices)
     def _(off):
         s = lax.rem(me + devices - off, devices)
@@ -221,7 +224,6 @@
     cg_copy = pltpu.make_async_copy(cg, cg_out, out_sem.at[0])
     cg_copy.start()
     for layer in reversed(range(1, layers)):
-        open_gate(layer)
         for rp in range(2):
             for copy in halos(layer, rp):
                 copy.wait_recv()
@@ -235,7 +237,6 @@
         part = pl.ds(start, count)
         return pltpu.make_async_copy(last.at[:, part], hid_out.at[:, part], out_sem.at[sem])
 
-    open_gate(0)
     pl.loop(2, quads)(finish)
     hid_copy(1, quads - 2, 1).start()
     for rp in range(2):

time: 59.4 us -> 58.4 us (0.983)
  Pallas kernels: 59.2 us -> 58.2 us
    pallas_call x1, Pallas kernels: 54.2 us -> 53.2 us  [per_device(): pl.pallas_call(functools.partial(kernel, dims), out_shape=[jax.ShapeDtype...]
where the time goes in v5:
time: 58.4 us; the launch traced here: 58.2 us
  Pallas kernels  58.2 us (100%)
    pallas_call x1, Pallas kernels, per_device(): pl.pallas_call(functools.partial(kernel, dims), out_shape=[jax.ShapeDtype...  53.2 us
    pallas_call x1, Pallas kernels, per_device(): pl.pallas_call(encode_kernel, out_shape=jax.ShapeDtypeStruct((levels, til...  4.96 us

profile of v5, /device:TPU:0, one launch (start us, length us, event | category | flops | bytes accessed | tf_op | source)
XLA Modules:
  0.0 58.2 jit_solution(854890408028161346)
XLA Ops:
  0.0 53.2 %shard_map.91 = (bf16[2,16,144,256]{3,2,1,0:T(8,128)(2,1)}, bf16[2,16,128,256]{3,2,1,0:T(8,128)(2,1)}) custom-call(bf16[128,512]{1,0:T(8,128)(2,1)} %resid.1, s32[2,512]{1,0:T(2,128)} %index.1, s32[1,32]{1,0:T(1,128)} %counts.1, f32[1,128]{1,0:T(1,128)} %bitcast.5, bf16[137,8,128]{2,1,0:T(8,128)(2,1)} %bitcast.3, bf16[137,128]{1,0:T(8,128)(2,1)} %dec.1, ...), custom_call_target="tpu_custom_call" | custom-call | tf_op jit(solution)/shard_map/pallas_call | solution.py:328
  53.2 5.0 %shard_map.92 = f32[137,64,128]{2,1,0:T(8,128)} custom-call(bf16[2,16,144,256]{3,2,1,0:T(8,128)(2,1)} %get-tuple-element.7.cg_in, bf16[2,16,128,256]{3,2,1,0:T(8,128)(2,1)} %get-tuple-element.8.hid_in, bf16[137,128]{1,0:T(8,128)(2,1)} %bitcast.4), custom_call_target="tpu_custom_call" | custom-call | tf_op jit(solution)/shard_map/pallas_call | solution.py:366
